TPU v7x, 256 devices: a whole 4x4x8 slice. The times are simulated.
256 devices in a mesh: src: 32 (over x, y, core), tgt: 8 (over z).
Axes of the slice: x: 4, y: 4, z: 8, core: 2. Of those that a mesh axis runs over, the one named last changes fastest.
Arguments:
- sources: float32 [32768, 128], P(('src', 'tgt')), may hold values from -3 to 3
- targets: float32 [32768, 128], P(('tgt', 'src')), may hold values from -0.6 to 0.6
- log_src_mass: float32 [32768], P('src'), may hold values from -1 to 1
- log_tgt_mass: float32 [32768], P('tgt'), may hold values from -1 to 1
Outputs:
- src_potential: float32 [32768], P('src')
- tgt_potential: float32 [32768], P('tgt')
All inputs are finite; a program needn't handle non-finite values.
Results may differ from a plain program's by a relative error of at most 0.0003.
Values sent between devices are 32-bit elements; how exact they have to be, the bound alone decides.
No kernel may reach another device: no remote copies, remote signals or barrier semaphores. Data moves between devices by JAX's collectives and lax.ppermute only.
A program may use at most 64 MiB of HBM per device.

v0:
```python
import jax
import jax.numpy as jnp
from jax import lax
from jax.sharding import PartitionSpec as P

ITERS = 3


eps = 0.05


def local(sources, targets, log_src_mass, log_tgt_mass):
    block = lax.all_gather(sources, "tgt", axis=0, tiled=True)
    src_sq = jnp.sum(block * block, axis=1)
    piece = lax.all_gather(targets, "src", axis=0, tiled=True)
    piece_sq = jnp.sum(piece * piece, axis=1)
    cross = jnp.dot(
        block, piece.T, precision=lax.Precision.HIGHEST, preferred_element_type=jnp.float32
    )
    cost = src_sq[:, None] + piece_sq[None, :] - 2.0 * cross
    tgt_potential = jnp.zeros(log_tgt_mass.shape, jnp.float32)
    src_potential = jnp.zeros(log_src_mass.shape, jnp.float32)
    for step in range(ITERS):
        expo = log_tgt_mass[None, :] + (tgt_potential[None, :] - cost) / eps
        peak = lax.pmax(jnp.max(expo, axis=1), "tgt")
        total = lax.psum(jnp.sum(jnp.exp(expo - peak[:, None]), axis=1), "tgt")
        src_potential = -eps * (peak + jnp.log(total))
        weigh = log_src_mass[:, None] + (src_potential[:, None] - cost) / eps
        peak = lax.pmax(jnp.max(weigh, axis=0), "src")
        total = lax.psum(jnp.sum(jnp.exp(weigh - peak[None, :]), axis=0), "src")
        tgt_potential = -eps * (peak + jnp.log(total))
    return (src_potential, tgt_potential)


def solution(mesh):
    in_specs = (P(("src", "tgt"), None), P(("tgt", "src"), None), P("src"), P("tgt"))
    out_specs = (P("src"), P("tgt"))
    return jax.shard_map(local, mesh=mesh, in_specs=in_specs, out_specs=out_specs, check_vma=False)
```

profile of v0, /device:TPU:1, one launch (start us, length us, event | category | flops | bytes accessed | tf_op | source)
XLA Modules:
  0.0 1016.8 jit_solution(7589589921469271728)
XLA Ops:
  7.2 0.0 all-gather.2.cloned.1.call-start
  7.2 0.7 all-gather.2.cloned.1.call-update
  7.9 24.0 %all_gather.6 = f32[1024,128]{1,0:T(8,128)S(1)} all-gather(f32[128,128]{1,0:T(8,128)} %param.4), channel_id=1, replica_groups=mesh['src'=32,'tgt'=8] {'tgt'}, dimensions={0}, use_global_device_ids=true | all-gather | bytes 589824 | tf_op jit(solution)/shard_map/all_gather | solution.py:13
  31.9 0.2 multiply_reduce_fusion.1
  32.1 31.5 %all-gather.2.cloned.1.call-done = f32[4096,128]{1,0:T(8,128)} async-done(((f32[128,128]{1,0:T(8,128)}), f32[4096,128]{1,0:T(8,128)}) %all-gather.2.cloned.1.call-update) | async-done | bytes 2097168 | tf_op jit(solution)/shard_map/all_gather | solution.py:15
  63.7 2.2 multiply_reduce_fusion
  65.9 0.0 copy-start
  65.9 20.3 %fusion = (f32[1024]{0:T(1024)S(1)}, f32[1024,4096]{1,0:T(8,128)}) fusion(f32[4096]{0:T(1024)} %param.7, f32[1024,128]{1,0:T(8,128)S(1)} %all_gather.6, f32[4096,128]{1,0:T(8,128)} %all-gather.2.cloned.1.call-done, f32[4096]{0:T(1024)S(1)} %multiply_reduce_fusion, f32[1024]{0:T(1024)S(1)} %multiply_reduce_fusion.1), kind=kOutput, calls=%fused_computation.13 | convolution fusion | flops 6471810048 | bytes 19439616 | tf_op jit(solution)/shard_map/dot_general | solution.py:17
  86.1 0.0 copy-start.1
  86.1 14.0 %pmax.42 = f32[1024]{0:T(1024)S(1)} all-reduce(f32[1024]{0:T(1024)S(1)} %get-tuple-element.2), channel_id=1, replica_groups=mesh['src'=32,'tgt'=8] {'tgt'}, use_global_device_ids=true, to_apply=%region_3.0 | all-reduce | flops 1024 | bytes 8192 | tf_op jit(solution)/shard_map/pmax | solution.py:25
  100.1 0.0 copy-done
  100.1 8.1 exponential_reduce_fusion.5
  108.2 11.2 %psum.42 = f32[1024]{0:T(1024)S(1)} all-reduce(f32[1024]{0:T(1024)S(1)} %exponential_reduce_fusion.5), channel_id=1, replica_groups=mesh['src'=32,'tgt'=8] {'tgt'}, use_global_device_ids=true, to_apply=%region_5.0 | all-reduce | flops 1024 | bytes 8192 | tf_op jit(solution)/shard_map/psum | solution.py:26
  119.4 0.0 copy-done.1
  119.5 9.1 fusion.1
  128.6 125.8 %pmax.43 = f32[4096]{0:T(1024)S(1)} all-reduce(f32[4096]{0:T(1024)S(1)} %fusion.1), channel_id=1, replica_groups=mesh['src'=32,'tgt'=8] {'src'}, use_global_device_ids=true, to_apply=%region_7.0 | all-reduce | flops 4096 | bytes 32768 | tf_op jit(solution)/shard_map/pmax | solution.py:29
  254.4 8.1 exponential_reduce_fusion.4
  262.5 124.0 %psum.43 = f32[4096]{0:T(1024)S(1)} all-reduce(f32[4096]{0:T(1024)S(1)} %exponential_reduce_fusion.4), channel_id=1, replica_groups=mesh['src'=32,'tgt'=8] {'src'}, use_global_device_ids=true, to_apply=%region_9.0 | all-reduce | flops 4096 | bytes 32768 | tf_op jit(solution)/shard_map/psum | solution.py:30
  386.4 8.0 fusion.2
  394.5 11.5 %pmax.44 = f32[1024]{0:T(1024)S(1)} all-reduce(f32[1024]{0:T(1024)S(1)} %fusion.2), channel_id=1, replica_groups=mesh['src'=32,'tgt'=8] {'tgt'}, use_global_device_ids=true, to_apply=%region_11.0 | all-reduce | flops 1024 | bytes 8192 | tf_op jit(solution)/shard_map/pmax | solution.py:25
  406.0 8.1 exponential_reduce_fusion.3
  414.2 11.4 %psum.44 = f32[1024]{0:T(1024)S(1)} all-reduce(f32[1024]{0:T(1024)S(1)} %exponential_reduce_fusion.3), channel_id=1, replica_groups=mesh['src'=32,'tgt'=8] {'tgt'}, use_global_device_ids=true, to_apply=%region_13.0 | all-reduce | flops 1024 | bytes 8192 | tf_op jit(solution)/shard_map/psum | solution.py:26
  425.6 9.1 fusion.3
  434.8 131.1 %pmax.45 = f32[4096]{0:T(1024)S(1)} all-reduce(f32[4096]{0:T(1024)S(1)} %fusion.3), channel_id=1, replica_groups=mesh['src'=32,'tgt'=8] {'src'}, use_global_device_ids=true, to_apply=%region_15.0 | all-reduce | flops 4096 | bytes 32768 | tf_op jit(solution)/shard_map/pmax | solution.py:29
  565.9 8.1 exponential_reduce_fusion.2
  574.0 123.8 %psum.45 = f32[4096]{0:T(1024)S(1)} all-reduce(f32[4096]{0:T(1024)S(1)} %exponential_reduce_fusion.2), channel_id=1, replica_groups=mesh['src'=32,'tgt'=8] {'src'}, use_global_device_ids=true, to_apply=%region_17.0 | all-reduce | flops 4096 | bytes 32768 | tf_op jit(solution)/shard_map/psum | solution.py:30
  697.8 8.0 fusion.4
  705.8 11.7 %pmax.46 = f32[1024]{0:T(1024)S(1)} all-reduce(f32[1024]{0:T(1024)S(1)} %fusion.4), channel_id=1, replica_groups=mesh['src'=32,'tgt'=8] {'tgt'}, use_global_device_ids=true, to_apply=%region_19.0 | all-reduce | flops 1024 | bytes 8192 | tf_op jit(solution)/shard_map/pmax | solution.py:25
  717.6 8.2 exponential_reduce_fusion.1
  725.7 11.4 %psum.46 = f32[1024]{0:T(1024)S(1)} all-reduce(f32[1024]{0:T(1024)S(1)} %exponential_reduce_fusion.1), channel_id=1, replica_groups=mesh['src'=32,'tgt'=8] {'tgt'}, use_global_device_ids=true, to_apply=%region_21.0 | all-reduce | flops 1024 | bytes 8192 | tf_op jit(solution)/shard_map/psum | solution.py:26
  737.2 0.0 copy-start.2
  737.2 9.1 fusion.5
  746.3 131.1 %pmax.47 = f32[4096]{0:T(1024)S(1)} all-reduce(f32[4096]{0:T(1024)S(1)} %fusion.5), channel_id=1, replica_groups=mesh['src'=32,'tgt'=8] {'src'}, use_global_device_ids=true, to_apply=%region_23.0 | all-reduce | flops 4096 | bytes 32768 | tf_op jit(solution)/shard_map/pmax | solution.py:29
  877.5 8.1 exponential_reduce_fusion
  885.6 0.0 copy-done.2
  885.6 123.8 %psum.47 = f32[4096]{0:T(1024)S(1)} all-reduce(f32[4096]{0:T(1024)S(1)} %exponential_reduce_fusion), channel_id=1, replica_groups=mesh['src'=32,'tgt'=8] {'src'}, use_global_device_ids=true, to_apply=%region_25.0 | all-reduce | flops 4096 | bytes 32768 | tf_op jit(solution)/shard_map/psum | solution.py:30
  1009.4 0.6 add_multiply_fusion
  (5 shorter events, 0.0 us)
Async XLA Ops:
  7.2 56.5 %all-gather.2.cloned.1.call-start = ((), (), s32[]{:S(2)}) async-start(), calls=%async_computation | async-start | bytes 2162688 | tf_op jit(solution)/shard_map/all_gather | solution.py:15
  65.9 34.3 %copy-start = (f32[4096]{0:T(1024)S(1)}, f32[4096]{0:T(1024)}, u32[]{:S(2)}) copy-start(f32[4096]{0:T(1024)} %param.7) | copy-start | bytes 49156
  86.1 33.3 %copy-start.1 = (f32[1024]{0:T(1024)S(1)}, f32[1024]{0:T(1024)}, u32[]{:S(2)}) copy-start(f32[1024]{0:T(1024)} %param.6) | copy-start | bytes 12292
  737.2 148.4 %copy-start.2 = (f32[1024]{0:T(1024)}, f32[1024]{0:T(1024)S(1)}, u32[]{:S(2)}) copy-start(f32[1024]{0:T(1024)S(1)} %add_multiply_fusion.3) | copy-start | bytes 12292
Sparse Core Ops, SparseCore 0:
  10.6 53.0 all-gather.1
where the time goes:
time: 1020 us
  blocking collectives  855 us (84%)
  other arithmetic  95.3 us (9%)
  waiting for transfers between devices  32.2 us (3%)
  matrix products  20.3 us (2%)
  between operations  14.1 us (1%)
    pmax x3, blocking collectives, local(): peak = lax.pmax(jnp.max(weigh, axis=0), 'src')  388 us
    psum x3, blocking collectives, local(): total = lax.psum(jnp.sum(jnp.exp(weigh - peak[None, :]), axis=0), 'src')  372 us
    pmax x3, blocking collectives, local(): peak = lax.pmax(jnp.max(expo, axis=1), 'tgt')  37.3 us
    psum x3, blocking collectives, local(): total = lax.psum(jnp.sum(jnp.exp(expo - peak[:, None]), axis=1), 'tgt')  34.1 us
    all_gather x1, waiting for transfers between devices, local(): piece = lax.all_gather(targets, 'src', axis=0, tiled=True)  31.5 us
    reduce_max x3, other arithmetic, local(): peak = lax.pmax(jnp.max(weigh, axis=0), 'src')  27.4 us
    reduce_sum x3, other arithmetic, local(): total = lax.psum(jnp.sum(jnp.exp(expo - peak[:, None]), axis=1), 'tgt')  24.4 us
    reduce_sum x3, other arithmetic, local(): total = lax.psum(jnp.sum(jnp.exp(weigh - peak[None, :]), axis=0), 'src')  24.3 us
  transfers between devices with their start and end apart: 1, of which 1 were waited for; matrix products, arithmetic and copies ran while one was open for 0% of the time, Pallas kernels for 0%

commit v1 on v0

v1 whole, which is shorter than its diff:
```python
import functools
import math

import jax
import jax.numpy as jnp
from jax import lax
from jax.experimental import pallas as pl
from jax.experimental.pallas import tpu as pltpu
from jax.sharding import Mesh
from jax.sharding import PartitionSpec as P

eps = 0.05
LOG2E = math.log2(math.e)
KAPPA = LOG2E / eps
SHIFT = 43.0
L = 128
B = 16
H = B // 2
N = B * L
F32 = jnp.float32
BF16 = jnp.bfloat16
VM = pl.BlockSpec(memory_space=pltpu.VMEM)
SM = pl.BlockSpec(memory_space=pltpu.SMEM)
VEC = (B, L)
PARTS = ((0, 0), (0, 1), (1, 0), (1, 1), (0, 2), (2, 0))


def rows_of(q):
    return pl.ds(pl.multiple_of(q * L, L), L)


def lanes_of(s):
    return pl.ds(s * L, L)


def fold(x, op):
    return op(x.reshape(-1, 8, L), axis=0)


def spread(vec, out_ref):
    turned = jnp.concatenate([vec, jnp.zeros((L - B, L), F32)], axis=0).T
    for q in range(B):
        out_ref[q * L : (q + 1) * L, :] = jnp.broadcast_to(turned[:, q : q + 1], (L, L))


def split3(x):
    a = x.astype(BF16)
    x = x - a.astype(F32)
    b = x.astype(BF16)
    x = x - b.astype(F32)
    return a, b, x.astype(BF16)


def start_kernel(
    core_ref, own_ref, other_ref, tgt_ref, lt_ref, ls_own_ref, ls_other_ref, z_ref, pay_ref, ls_ref, s6, t6, beta
):
    core = core_ref[0]
    ls_ref[pl.ds(pl.multiple_of(core * H, H), H), :] = ls_own_ref[...]
    ls_ref[pl.ds(pl.multiple_of((1 - core) * H, H), H), :] = ls_other_ref[...]
    for half, ref in ((core, own_ref), (1 - core, other_ref)):
        for q in range(H):
            parts = split3(ref[q * L : (q + 1) * L, :] * (2.0 * KAPPA))
            for c, (a, _) in enumerate(PARTS):
                s6[rows_of(half * H + q), c * L : (c + 1) * L] = parts[a]
    for q in range(B):
        t = tgt_ref[q * L : (q + 1) * L, :].T
        beta[q : q + 1, :] = LOG2E * lt_ref[q : q + 1, :] - KAPPA * jnp.sum(t * t, axis=0, keepdims=True)
        parts = split3(t)
        for c, (_, b) in enumerate(PARTS):
            t6[c * L : (c + 1) * L, q * L : (q + 1) * L] = parts[b]

    for c in range(0, B, 2):
        g = jnp.dot(s6[...], t6[:, c * L : (c + 2) * L], preferred_element_type=F32)
        for s in range(2):
            z_ref[:, lanes_of(c + s)] = g[:, s * L : (s + 1) * L] + beta[c + s : c + s + 1, :]

    def stats(q, _):
        rows = rows_of(q)
        peak = z_ref[rows, lanes_of(0)]
        for s in range(1, B):
            peak = jnp.maximum(peak, z_ref[rows, lanes_of(s)])
        total = jnp.zeros((L, L), F32)
        for s in range(B):
            total = total + jnp.exp2(z_ref[rows, lanes_of(s)] - peak)
        peak = peak.T
        top = jnp.max(peak, axis=0, keepdims=True)
        pay_ref[pl.ds(q, 1), :] = top + jnp.log2(jnp.sum(total.T * jnp.exp2(peak - top), axis=0, keepdims=True))
        return 0

    lax.fori_loop(0, B, stats, 0, unroll=4)


def merge(got_ref):
    got = [got_ref[d] for d in range(B)]
    top = functools.reduce(jnp.maximum, got)
    return top + jnp.log2(functools.reduce(jnp.add, [jnp.exp2(x - top) for x in got]))


def add_up(got_ref):
    return functools.reduce(jnp.add, [got_ref[d] for d in range(B)])


def cols_kernel(z_ref, got_ref, ls_ref, e_ref, pay_ref, m_ref, alpha_ref, wide):
    alpha = LOG2E * ls_ref[...] - merge(got_ref)
    alpha_ref[...] = alpha
    spread(alpha, wide)

    def highest(q, peak):
        a = wide[rows_of(q), :]
        return tuple(jnp.maximum(peak[s], fold(z_ref[rows_of(q), lanes_of(s)] + a, jnp.max)) for s in range(B))

    peak = lax.fori_loop(0, B, highest, (jnp.full((8, L), -1e30, F32),) * B, unroll=2)
    for s in range(B):
        m_ref[s : s + 1, :] = jnp.max(peak[s], axis=0, keepdims=True)

    ahead = 3
    for c in range(0, B, H):

        def weigh(q, total, c=c):
            rows = pl.ds(pl.multiple_of(q * (L // 2), L // 2), L // 2)
            a = wide[rows, :] + SHIFT
            held = [z_ref[rows, lanes_of(c + s)] for s in range(ahead)]
            out = []
            for s in range(H):
                if s + ahead < H:
                    held.append(z_ref[rows, lanes_of(c + s + ahead)])
                e = jnp.exp2((held[s] + a) - m_ref[c + s : c + s + 1, :])
                e_ref[rows, lanes_of(c + s)] = e
                out.append(total[s] + fold(e, jnp.sum))
            return tuple(out)

        total = lax.fori_loop(0, 2 * B, weigh, (jnp.zeros((8, L), F32),) * H, unroll=2)
        for s in range(H):
            one = slice(c + s, c + s + 1)
            pay_ref[one, :] = m_ref[one, :] + (jnp.log2(jnp.sum(total[s], axis=0, keepdims=True)) - SHIFT)


def row_sums(e_ref, v_ref, pay_ref):
    def body(q, _):
        total = jnp.zeros((L, L), F32)
        for s in range(B):
            total = total + e_ref[rows_of(q), lanes_of(s)] * v_ref[s : s + 1, :]
        pay_ref[pl.ds(q, 1), :] = jnp.sum(total.T, axis=0, keepdims=True)
        return 0

    lax.fori_loop(0, B, body, 0, unroll=8)


def col_sums(e_ref, v0_ref, pay_ref, wide):
    def body(q, carry):
        u = wide[rows_of(q), :]
        return tuple(carry[s] + fold(e_ref[rows_of(q), lanes_of(s)] * u, jnp.sum) for s in range(B))

    done = lax.fori_loop(0, B, body, (jnp.zeros((8, L), F32),) * B, unroll=8)
    for s in range(B):
        pay_ref[s : s + 1, :] = v0_ref[s : s + 1, :] * jnp.sum(done[s], axis=0, keepdims=True)


def first_row_kernel(e_ref, got_ref, m_ref, lt_ref, pay_ref, n_ref, v0_ref):
    n = merge(got_ref)
    n_ref[...] = n
    v0_ref[...] = jnp.exp2(m_ref[...] - n + (LOG2E * lt_ref[...] + SHIFT))
    row_sums(e_ref, v0_ref, pay_ref)


def col_kernel(e_ref, got_ref, ls_ref, v0_ref, pay_ref, wide):
    spread(jnp.exp2(LOG2E * ls_ref[...]) / add_up(got_ref), wide)
    col_sums(e_ref, v0_ref, pay_ref, wide)


def row_kernel(e_ref, got_ref, lt_ref, v0_ref, pay_ref, v):
    v[...] = v0_ref[...] * (jnp.exp2(LOG2E * lt_ref[...]) / add_up(got_ref))
    row_sums(e_ref, v, pay_ref)


def last_kernel(core_ref, e_ref, got_ref, ls_ref, v0_ref, alpha_ref, sq_ref, pay_ref, f_ref, wide, total):
    total[...] = add_up(got_ref)
    own = pl.ds(pl.multiple_of(core_ref[0] * H, H), H)
    f_ref[...] = sq_ref[...] - (eps / LOG2E) * (jnp.log2(total[own, :]) - 2.0 * SHIFT - alpha_ref[own, :])
    spread(jnp.exp2(LOG2E * ls_ref[...]) / total[...], wide)
    col_sums(e_ref, v0_ref, pay_ref, wide)


def call(kernel, outs, *args, scratch=(), limit=8, aliases=None):
    return pl.pallas_call(
        kernel,
        out_shape=[pltpu.VMEM(shape, F32) for shape in outs],
        in_specs=[SM if x.dtype == jnp.int32 else VM for x in args],
        out_specs=[VM] * len(outs),
        scratch_shapes=scratch,
        input_output_aliases=aliases or {},
        compiler_params=pltpu.CompilerParams(vmem_limit_bytes=limit * 2**20),
        name=kernel.__name__,
    )(*args)


def share(x, axes, count):
    return lax.all_to_all(jnp.broadcast_to(x[None], (count,) + x.shape), axes, 0, 0, tiled=True)


def over_rows(x):
    return share(x, ("c", "z"), B)


def over_cols(x):
    return share(x, ("x", "y"), B)


def swap(x):
    return lax.ppermute(x, "c", [(0, 1), (1, 0)])


def local(sources, targets, log_src_mass, log_tgt_mass):
    c = lax.axis_index("c")
    core = c.reshape(1)
    ls = log_src_mass.reshape(H, L)
    lt = lax.dynamic_index_in_dim(log_tgt_mass.reshape(B, 2, L), c, 1, keepdims=False)
    own = share(sources, "z", H).reshape(N // 2, L)
    own, sq = lax.optimization_barrier((own, jnp.sum(own * own, axis=1).reshape(H, L)))
    tgt = over_cols(targets).reshape(N, L)
    wide = pltpu.VMEM((N, L), F32)
    bits = [pltpu.VMEM((N, 6 * L), BF16), pltpu.VMEM((6 * L, N), BF16), pltpu.VMEM(VEC, F32)]
    z, pay, ls = call(
        start_kernel, [(N, N), VEC, VEC], core, own, swap(own), tgt, lt, ls, swap(ls), scratch=bits, limit=24
    )
    e, pay, m, alpha = call(cols_kernel, [(N, N), VEC, VEC, VEC], z, over_rows(pay), ls, scratch=[wide], aliases={0: 0})
    pay, n, v0 = call(first_row_kernel, [VEC, VEC, VEC], e, over_cols(pay), m, lt)
    (pay,) = call(col_kernel, [VEC], e, over_rows(pay), ls, v0, scratch=[wide])
    (pay,) = call(row_kernel, [VEC], e, over_cols(pay), lt, v0, scratch=[pltpu.VMEM(VEC, F32)])
    pay, f = call(
        last_kernel, [VEC, (H, L)], core, e, over_rows(pay), ls, v0, alpha, sq, scratch=[wide, pltpu.VMEM(VEC, F32)]
    )
    total = jnp.sum(over_cols(pay), axis=0)
    g = -eps * ((jnp.log2(total) + n) / LOG2E - 2.0 * lt)
    g = lax.all_gather(g, "c").transpose(1, 0, 2).reshape(2 * N)
    return f.reshape(N // 2), g


def solution(mesh):
    grid = Mesh(mesh.devices.reshape(4, 4, 2, 8), ("x", "y", "c", "z"))
    src, tgt = ("x", "y", "c"), "z"
    in_specs = (P((*src, tgt), None), P((tgt, *src), None), P(src), P(tgt))
    return jax.shard_map(local, mesh=grid, in_specs=in_specs, out_specs=(P(src), P(tgt)), check_vma=False)
```

time: 1020 us -> 148 us (0.15)
  blocking collectives: 855 us -> 88.2 us
  other arithmetic: 95.3 us -> 0.24 us
  Pallas kernels: 0 us -> 22.7 us
  matrix products: 20.3 us -> 0 us
  waiting for transfers between devices: 32.2 us -> 17.3 us
  between operations: 14.1 us -> 0.77 us
  starting transfers between devices: 0.04 us -> 13.2 us
    pmax x6 -> x0, blocking collectives: 425 us -> none  [the longest x3 388 us: local(): peak = lax.pmax(jnp.max(weigh, axis=0), 'src')]
    psum x6 -> x0, blocking collectives: 406 us -> none  [the longest x3 372 us: local(): total = lax.psum(jnp.sum(jnp.exp(weigh - peak[None, :]), axis=0), 'src')]
    all_to_all x0 -> x6, blocking collectives: none -> 84.1 us  [share(): lax.all_to_all(jnp.broadcast_to(x[None], (count,) + x.shape), axes, 0, 0,...]
    reduce_sum x8 -> x2, other arithmetic: 51.1 us -> 0.23 us  [the longest x1 0.21 us: local(): jnp.sum(own * own, axis=1).reshape(H, L)]
    reduce_max x5 -> x0, other arithmetic: 43.5 us -> none  [the longest x3 27.4 us: local(): peak = lax.pmax(jnp.max(weigh, axis=0), 'src')]
    all_gather x1 -> x0, waiting for transfers between devices: 31.5 us -> none  [local(): piece = lax.all_gather(targets, 'src', axis=0, tiled=True)]
    pallas_call x0 -> x6, Pallas kernels: none -> 22.7 us  [call(): pl.pallas_call(kernel, out_shape=[pltpu.VMEM(shape, F32) for shape in out...]
    dot_general x1 -> x0, matrix products: 20.3 us -> none  [local(): jnp.dot(block, piece.T, precision=lax.Precision.HIGHEST, preferred_elemen...]
  transfers between devices with their start and end apart: 1 -> 4, of which waited for: 1 -> 3; matrix products, arithmetic and copies ran while one was open for 0% -> 1% of each run, Pallas kernels for 0% -> 0%
where the time goes in v1:
time: 148 us
  blocking collectives  88.2 us (60%)
  Pallas kernels  22.7 us (15%)
  waiting for transfers between devices  17.3 us (12%)
  starting transfers between devices  13.2 us (9%)
  local copies, waits for them, and re-layouts  5.42 us (4%)
    all_to_all x6, blocking collectives, share(): lax.all_to_all(jnp.broadcast_to(x[None], (count,) + x.shape), axes, 0, 0,...  84.1 us
    pallas_call x6, Pallas kernels, call(): pl.pallas_call(kernel, out_shape=[pltpu.VMEM(shape, F32) for shape in out...  22.7 us
    all_to_all x2, waiting for transfers between devices, share(): lax.all_to_all(jnp.broadcast_to(x[None], (count,) + x.shape), axes, 0, 0,...  15.6 us
    all_to_all x2, starting transfers between devices, share(): lax.all_to_all(jnp.broadcast_to(x[None], (count,) + x.shape), axes, 0, 0,...  10.3 us
    all_gather x1, blocking collectives, local(): g = lax.all_gather(g, 'c').transpose(1, 0, 2).reshape(2 * N)  4.07 us
    broadcast_in_dim x8, local copies, waits for them, and re-layouts, share(): jnp.broadcast_to(x[None], (count,) + x.shape)  3.5 us
  transfers between devices with their start and end apart: 4, of which 3 were waited for; matrix products, arithmetic and copies ran while one was open for 1% of the time, Pallas kernels for 0%

profile of v1, /device:TPU:1, one launch (start us, length us, event | category | flops | bytes accessed | tf_op | source)
XLA Modules:
  0.0 147.8 jit_solution(17944466407284972221)
XLA Ops:
  0.6 0.0 copy-start
  0.6 0.9 broadcast_in_dim.16
  1.5 24.8 %all_to_all.40 = f32[8,128,128]{2,1,0:T(8,128)S(1)} all-to-all(f32[8,128,128]{2,1,0:T(8,128)S(1)} %broadcast_in_dim.16), channel_id=1, replica_groups=mesh['x'=4,'y'=4,'c'=2,'z'=8] {'z'}, dimensions={0} | all-to-all | bytes 1048576 | tf_op jit(solution)/shard_map/all_to_all | solution.py:198
  26.3 1.9 %broadcast_in_dim.17 = f32[16,128,128]{2,1,0:T(8,128)} broadcast(f32[128,128]{1,0:T(8,128)} %param.5), dimensions={1,2} | broadcast | bytes 1114112 | tf_op jit(solution)/shard_map/broadcast_in_dim | solution.py:198
  28.2 6.8 %all-to-all-start.1 = ((f32[16,128,128]{2,1,0:T(8,128)}), f32[16,128,128]{2,1,0:T(8,128)S(1)}, u32[]{:S(2)}, u32[]{:S(2)}) async-start(f32[16,128,128]{2,1,0:T(8,128)} %broadcast_in_dim.17), calls=%async_computation.1 | async-start | bytes 2097152 | tf_op jit(solution)/shard_map/all_to_all | solution.py:198
  35.0 0.2 multiply_reduce_fusion.sq_ref
  35.2 2.8 %collective-permute-start = (f32[1024,128]{1,0:T(8,128)S(1)}, f32[1024,128]{1,0:T(8,128)S(1)}, u32[]{:S(2)}, u32[]{:S(2)}) collective-permute-start(f32[1024,128]{1,0:T(8,128)S(1)} %bitcast.13), channel_id=1, source_target_pairs={{0,8},{8,0},{1,9},{9,1},{2,10},{10,2},{3,11},{11,3},{4,12},{12,4},... | collective-permute-start | bytes 1572872 | tf_op jit(solution)/shard_map/ppermute | solution.py:210
  38.0 0.1 collective-permute-start.1
  38.1 0.0 copy-done
  38.2 1.6 %collective-permute-done.1.ls_other_ref = f32[8,128]{1,0:T(8,128)S(1)} collective-permute-done((f32[8,128]{1,0:T(8,128)}, f32[8,128]{1,0:T(8,128)S(1)}, u32[]{:S(2)}, u32[]{:S(2)}) %collective-permute-start.1) | collective-permute-done | bytes 4128 | tf_op jit(solution)/shard_map/ppermute | solution.py:210
  39.8 9.6 %all-to-all-done.1 = f32[16,128,128]{2,1,0:T(8,128)S(1)} async-done(((f32[16,128,128]{2,1,0:T(8,128)}), f32[16,128,128]{2,1,0:T(8,128)S(1)}, u32[]{:S(2)}, u32[]{:S(2)}) %all-to-all-start.1) | async-done | bytes 1048608 | tf_op jit(solution)/shard_map/all_to_all | solution.py:198
  49.4 0.0 collective-permute-done.other_ref
  49.4 0.0 copy-start.1
  49.4 0.7 copy-done.1
  50.1 10.4 %start_kernel.1 = (f32[2048,2048]{1,0:T(8,128)S(1)}, f32[16,128]{1,0:T(8,128)S(1)}, f32[16,128]{1,0:T(8,128)S(1)}) custom-call(s32[1]{0:T(128)} %bitcast.core_ref, f32[1024,128]{1,0:T(8,128)S(1)} %bitcast.14, f32[1024,128]{1,0:T(8,128)S(1)} %collective-permute-done.other_ref, f32[2048,128]{1,0:T(8,128)S(1)} %bitcast.15, f32[16,128]{1,0:T(8,128)S(1)} %bitcast.16, ...), custom_call_target="tpu_custom_call" | custom-call | tf_op jit(solution)/shard_map/start_kernel/pallas_call | solution.py:185
  60.5 14.0 %all_to_all.41.got_ref = f32[16,16,128]{2,1,0:T(8,128)S(1)} all-to-all(f32[16,16,128]{2,1,0:T(8,128)S(1)} %broadcast_in_dim.18), channel_id=1, replica_groups=mesh['x'=4,'y'=4,'c'=2,'z'=8] {'c','z'}, dimensions={0} | all-to-all | bytes 262144 | tf_op jit(solution)/shard_map/all_to_all | solution.py:198
  74.6 6.0 %cols_kernel.1 = (f32[2048,2048]{1,0:T(8,128)S(1)}, f32[16,128]{1,0:T(8,128)S(1)}, f32[16,128]{1,0:T(8,128)S(1)}, f32[16,128]{1,0:T(8,128)S(1)}) custom-call(f32[2048,2048]{1,0:T(8,128)S(1)} %get-tuple-element.17.z_ref, f32[16,16,128]{2,1,0:T(8,128)S(1)} %all_to_all.41.got_ref, f32[16,128]{1,0:T(8,128)S(1)} %get-tuple-element.19.ls_ref), custom_call_target="tpu_custom_call", output_to_operand_aliasing={{0}: (0, {})} | custom-call | tf_op jit(solution)/shard_map/cols_kernel/pallas_call | solution.py:185
  80.6 9.4 %all_to_all.42.got_ref = f32[16,16,128]{2,1,0:T(8,128)S(1)} all-to-all(f32[16,16,128]{2,1,0:T(8,128)S(1)} %broadcast_in_dim.19), channel_id=1, replica_groups=mesh['x'=4,'y'=4,'c'=2,'z'=8] {'x','y'}, dimensions={0} | all-to-all | bytes 262144 | tf_op jit(solution)/shard_map/all_to_all | solution.py:198
  90.0 1.4 first_row_kernel.1
  91.4 13.0 %all_to_all.43.got_ref = f32[16,16,128]{2,1,0:T(8,128)S(1)} all-to-all(f32[16,16,128]{2,1,0:T(8,128)S(1)} %broadcast_in_dim.20), channel_id=1, replica_groups=mesh['x'=4,'y'=4,'c'=2,'z'=8] {'c','z'}, dimensions={0} | all-to-all | bytes 262144 | tf_op jit(solution)/shard_map/all_to_all | solution.py:198
  104.4 1.8 %col_kernel.1 = f32[16,128]{1,0:T(8,128)S(1)} custom-call(f32[2048,2048]{1,0:T(8,128)S(1)} %get-tuple-element.20.e_ref, f32[16,16,128]{2,1,0:T(8,128)S(1)} %all_to_all.43.got_ref, f32[16,128]{1,0:T(8,128)S(1)} %get-tuple-element.19.ls_ref, f32[16,128]{1,0:T(8,128)S(1)} %get-tuple-element.24.v0_ref), custom_call_target="tpu_custom_call" | custom-call | tf_op jit(solution)/shard_map/col_kernel/pallas_call | solution.py:185
  106.2 9.8 %all_to_all.44.got_ref = f32[16,16,128]{2,1,0:T(8,128)S(1)} all-to-all(f32[16,16,128]{2,1,0:T(8,128)S(1)} %broadcast_in_dim.21), channel_id=1, replica_groups=mesh['x'=4,'y'=4,'c'=2,'z'=8] {'x','y'}, dimensions={0} | all-to-all | bytes 262144 | tf_op jit(solution)/shard_map/all_to_all | solution.py:198
  116.0 1.4 row_kernel.1
  117.4 13.0 %all_to_all.45.got_ref = f32[16,16,128]{2,1,0:T(8,128)S(1)} all-to-all(f32[16,16,128]{2,1,0:T(8,128)S(1)} %broadcast_in_dim.22), channel_id=1, replica_groups=mesh['x'=4,'y'=4,'c'=2,'z'=8] {'c','z'}, dimensions={0} | all-to-all | bytes 262144 | tf_op jit(solution)/shard_map/all_to_all | solution.py:198
  130.4 1.8 %last_kernel.1 = (f32[16,128]{1,0:T(8,128)S(1)}, f32[8,128]{1,0:T(8,128)S(1)}) custom-call(s32[1]{0:T(128)} %bitcast.core_ref, f32[2048,2048]{1,0:T(8,128)S(1)} %get-tuple-element.20.e_ref, f32[16,16,128]{2,1,0:T(8,128)S(1)} %all_to_all.45.got_ref, f32[16,128]{1,0:T(8,128)S(1)} %get-tuple-element.19.ls_ref, f32[16,128]{1,0:T(8,128)S(1)} %get-tuple-element.24.v0_ref, ...), custom_call_target="tpu_custom_call" | custom-call | tf_op jit(solution)/shard_map/last_kernel/pallas_call | solution.py:185
  132.2 0.7 broadcast_in_dim.23
  132.9 3.5 %all-to-all-start.7 = ((f32[16,16,128]{2,1,0:T(8,128)}), f32[16,16,128]{2,1,0:T(8,128)S(1)}, u32[]{:S(2)}, u32[]{:S(2)}) async-start(f32[16,16,128]{2,1,0:T(8,128)} %broadcast_in_dim.23), calls=%async_computation.7 | async-start | bytes 262144 | tf_op jit(solution)/shard_map/all_to_all | solution.py:198
  136.4 0.6 copy.10
  137.0 6.0 %all-to-all-done.7 = f32[16,16,128]{2,1,0:T(8,128)S(1)} async-done(((f32[16,16,128]{2,1,0:T(8,128)}), f32[16,16,128]{2,1,0:T(8,128)S(1)}, u32[]{:S(2)}, u32[]{:S(2)}) %all-to-all-start.7) | async-done | bytes 131104 | tf_op jit(solution)/shard_map/all_to_all | solution.py:198
  143.1 4.1 %all-gather = f32[32,128]{1,0:T(8,128)S(1)} all-gather(f32[16,128]{1,0:T(8,128)S(1)} %subtract_multiply_fusion), channel_id=2, replica_groups=mesh['x'=4,'y'=4,'c'=2,'z'=8] {'c'}, dimensions={0}, use_global_device_ids=true | all-gather | bytes 24576 | tf_op jit(solution)/shard_map/all_gather | solution.py:235
  147.1 0.6 copy.8
  (8 shorter events, 0.1 us)
Async XLA Ops:
  0.6 37.5 %copy-start = (f32[4096]{0:T(1024)S(1)}, f32[4096]{0:T(1024)}, u32[]{:S(2)}) copy-start(f32[4096]{0:T(1024)} %param.7) | copy-start | bytes 49156
  28.2 21.2 %all-to-all-start.1 = ((f32[16,128,128]{2,1,0:T(8,128)}), f32[16,128,128]{2,1,0:T(8,128)S(1)}, u32[]{:S(2)}, u32[]{:S(2)}) async-start(f32[16,128,128]{2,1,0:T(8,128)} %broadcast_in_dim.17), calls=%async_computation.1 | async-start | bytes 2097152 | tf_op jit(solution)/shard_map/all_to_all | solution.py:198
  35.2 14.2 %collective-permute-start = (f32[1024,128]{1,0:T(8,128)S(1)}, f32[1024,128]{1,0:T(8,128)S(1)}, u32[]{:S(2)}, u32[]{:S(2)}) collective-permute-start(f32[1024,128]{1,0:T(8,128)S(1)} %bitcast.13), channel_id=1, source_target_pairs={{0,8},{8,0},{1,9},{9,1},{2,10},{10,2},{3,11},{11,3},{4,12},{12,4},... | collective-permute-start | bytes 1572872 | tf_op jit(solution)/shard_map/ppermute | solution.py:210
  38.0 1.8 %collective-permute-start.1 = (f32[8,128]{1,0:T(8,128)}, f32[8,128]{1,0:T(8,128)S(1)}, u32[]{:S(2)}, u32[]{:S(2)}) collective-permute-start(f32[8,128]{1,0:T(8,128)} %bitcast.20), channel_id=1, source_target_pairs={{0,8},{8,0},{1,9},{9,1},{2,10},{10,2},{3,11},{11,3},{4,12},{12,4},... | collective-permute-start | bytes 12296 | tf_op jit(solution)/shard_map/ppermute | solution.py:210
  49.4 0.7 copy-start.1
  132.9 10.1 %all-to-all-start.7 = ((f32[16,16,128]{2,1,0:T(8,128)}), f32[16,16,128]{2,1,0:T(8,128)S(1)}, u32[]{:S(2)}, u32[]{:S(2)}) async-start(f32[16,16,128]{2,1,0:T(8,128)} %broadcast_in_dim.23), calls=%async_computation.7 | async-start | bytes 262144 | tf_op jit(solution)/shard_map/all_to_all | solution.py:198
